TPU v7x, 32 devices: a whole 2x2x4 slice. The times are simulated.
32 devices in a mesh: dp: 8 (over z, core), tensor: 4 (over y, x).
Axes of the slice: x: 2, y: 2, z: 4, core: 2. Of those that a mesh axis runs over, the one named last changes fastest.
Arguments:
- features: bfloat16 [2560, 2048], P(('dp', 'tensor')), may hold values from -6 to 6
- w_hidden: bfloat16 [2048, 2048], P(None, 'tensor'), may hold values from -0.125 to 0.125
- w_embed: bfloat16 [2048, 768], P('tensor'), may hold values from -0.125 to 0.125
- members: bfloat16 [8, 512, 768], P('dp', 'tensor'), may hold values from -6 to 6
- doc_owner: int32 [2560, 1], P('dp'), may hold values from 0 to 7; in each aligned block of 80 rows (0 to 79, 80 to 159, ...) at most 20 rows name the same one
- doc_local: int32 [2560], P('dp'), may hold values from 0 to 15
- member_cluster: int32 [8, 512], P('dp', 'tensor'), may hold values from 0 to 15, never falling along the last dimension, each value on 1 to 48 neighbouring positions
- member_valid: int32 [8, 512], P('dp', 'tensor'), may hold values 0 or 1
Outputs:
- best: float32 [2560], P(('dp', 'tensor'))
Inputs may be any that keep to these rules, and one draw needn't show every extreme that they name: Among the 80 documents of one device (aligned blocks of doc_owner's rows, in the order of dp then tensor) no owner is named more than 20 times; some owner is named exactly 20 times. `member_cluster`: along each owner's row the clusters never fall; every cluster has 1 to 48 slots.
All inputs are finite; a program needn't handle non-finite values. No bound on the sum of `member_valid` on one device may be relied on, other than what follows from the above.
Results may differ from a plain program's by a relative error of at most 0.013.
Values may be sent and summed in bfloat16 or wider, within the bound.
A program may use at most 64 MiB of HBM per device.

v0:
```python
import functools
import math

import jax
import jax.numpy as jnp
from jax import lax
from jax.experimental import pallas as pl
from jax.experimental.pallas import tpu as pltpu
from jax.sharding import PartitionSpec as P

EPSILON = 1e-06
MESH = pl.DeviceIdType.MESH
F32 = jnp.float32
BF16 = jnp.bfloat16
LOWEST = -1e30
CHUNKS = 2


def iota(shape, dim):
    return lax.broadcasted_iota(jnp.int32, shape, dim).astype(F32)


def to_column(row, size):
    eye = iota((size, size), 0) == iota((size, size), 1)
    return jnp.sum(jnp.where(eye, row, 0.0), axis=1, keepdims=True)


def to_row(column, size):
    eye = iota((size, size), 0) == iota((size, size), 1)
    return jnp.sum(jnp.where(eye, column, 0.0), axis=0, keepdims=True)


class Sizes:
    def __init__(self, n_dp, n_tensor, rows, hid, width, emb, members):
        self.n_dp, self.n_tensor = n_dp, n_tensor
        self.rows, self.hid, self.width, self.emb, self.members = rows, hid, width, emb, members
        self.nx = max(d for d in range(1, math.isqrt(n_tensor) + 1) if n_tensor % d == 0)
        self.ny = n_tensor // self.nx
        shifts = [(x, y) for y in range(self.ny) for x in range(self.nx)]
        self.shifts = sorted(shifts, key=lambda xy: ((xy[0] > 0) + (xy[1] > 0), xy[1], xy[0]))
        self.along_x = [j for j, (x, y) in enumerate(self.shifts) if x and not y]
        self.along_y = [j for j, (x, y) in enumerate(self.shifts) if y and not x]
        self.far = [j for j, (x, y) in enumerate(self.shifts) if x and y]
        self.cap = min(rows, max(2, 2 * rows // n_dp))
        self.whole = self.cap // 16 * 16
        self.rest = self.cap - self.whole
        self.cols = emb // CHUNKS
        self.tiles = self.cols // 128
        self.folded = -(-self.rest * self.tiles // 16) * 16
        self.block = self.whole * self.tiles + self.folded
        self.slots = n_dp * self.cap
        self.lanes = -(-self.slots // 128) * 128


def kernel(
    z,
    features,
    w_hidden,
    w_embed,
    members,
    hbm_owner,
    hbm_local,
    hbm_cluster,
    hbm_valid,
    best,
    feat,
    w1,
    w2,
    raw,
    doc_owner,
    doc_local,
    member_cluster,
    member_valid,
    unit,
    member_tag,
    sums_out,
    sums_in,
    docs_out,
    docs_in,
    tags_out,
    tags_in,
    answer_out,
    answer_in,
    local_sem,
    feat_send,
    feat_recv,
    unit_send,
    unit_recv,
    mtag_send,
    mtag_recv,
    sums_send,
    sums_recv,
    docs_send,
    docs_recv,
    tags_send,
    tags_recv,
    answer_send,
    answer_recv,
):
    p = lax.axis_index("dp")
    t = lax.axis_index("tensor")
    tx, ty = lax.rem(t, z.nx), lax.div(t, z.nx)
    half = z.hid // 2
    sent = []

    def forward_of(j):
        dx, dy = z.shifts[j]
        return lax.rem(ty + dy, z.ny) * z.nx + lax.rem(tx + dx, z.nx)

    def source_of(j):
        dx, dy = z.shifts[j]
        return lax.rem(ty + z.ny - dy, z.ny) * z.nx + lax.rem(tx + z.nx - dx, z.nx)

    def remote(src, dst, send, recv, **device):
        copy = pltpu.make_async_remote_copy(
            src_ref=src, dst_ref=dst, send_sem=send, recv_sem=recv, device_id=device,
            device_id_type=MESH,
        )
        copy.start()
        sent.append(copy)
        return copy

    barrier = pltpu.get_barrier_semaphore()
    for j in range(1, z.n_tensor):
        pl.semaphore_signal(barrier, inc=1, device_id={"tensor": forward_of(j)}, device_id_type=MESH)
    for k in range(1, z.n_dp):
        pl.semaphore_signal(
            barrier, inc=1, device_id={"dp": lax.rem(p + k, z.n_dp)}, device_id_type=MESH
        )

    own = [
        pltpu.make_async_copy(features.at[:, pl.ds(h * half, half)], feat.at[h, 0], local_sem.at[h])
        for h in (0, 1)
    ]
    load_w1 = [
        pltpu.make_async_copy(
            w_hidden.at[pl.ds(h * half, half)], w1.at[pl.ds(h * half, half)], local_sem.at[2 + h]
        )
        for h in (0, 1)
    ]
    load_w2 = pltpu.make_async_copy(w_embed, w2, local_sem.at[4])
    load_members = pltpu.make_async_copy(members.at[0], raw, local_sem.at[5])
    load_small = [
        pltpu.make_async_copy(src, dst, local_sem.at[6 + i])
        for i, (src, dst) in enumerate(
            (
                (hbm_owner, doc_owner),
                (hbm_local, doc_local),
                (hbm_cluster, member_cluster),
                (hbm_valid, member_valid),
            )
        )
    ]
    for copy in (*load_small, *own, *load_w1, load_w2, load_members):
        copy.start()

    pl.semaphore_wait(barrier, z.n_tensor - 1 + z.n_dp - 1)

    feat_copy = {}

    def send_feature(h, j, src, target):
        feat_copy[h, j] = remote(
            src, feat.at[h, j], feat_send.at[h, j], feat_recv.at[h, j], tensor=forward_of(target)
        )

    along_x, along_y, far = z.along_x, z.along_y, z.far

    def corner(x, y):
        return z.shifts.index((z.shifts[x][0], z.shifts[y][1]))

    for first in (0, 1):
        for j in along_x:
            h = first
            send_feature(h, j, features.at[:, pl.ds(h * half, half)], j)
        for j in along_y:
            h = 1 - first
            send_feature(h, j, features.at[:, pl.ds(h * half, half)], j)

    for copy in load_small:
        copy.wait()
    rows, wide = z.rows, doc_owner.shape[1]
    mine = iota((rows, wide), 1) == iota((rows, wide), 0) + (t * rows).astype(F32)
    owner = jnp.sum(jnp.where(mine, doc_owner[...].astype(F32), 0.0), axis=1, keepdims=True)
    local = jnp.sum(jnp.where(mine, doc_local[...].reshape(1, wide).astype(F32), 0.0), axis=1, keepdims=True)
    step = owner - p.astype(F32)
    step = jnp.where(step < 0.0, step + float(z.n_dp), step)
    step_row = to_row(step, rows)
    same = step == step_row
    above = iota((rows, rows), 0)
    across = iota((rows, rows), 1)
    rank = jnp.sum(jnp.where(same & (across < above), 1.0, 0.0), axis=1, keepdims=True)
    rank_row = jnp.sum(jnp.where(same & (above < across), 1.0, 0.0), axis=0, keepdims=True)
    place = jnp.where(
        rank < float(z.whole),
        step * float(z.whole) + rank,
        float(z.n_dp * z.whole) + step * float(z.rest) + rank - float(z.whole),
    )
    placed = iota((rows, z.lanes), 1) == place
    step_hot = jnp.where(iota((z.n_dp, rows), 0) == step_row, 1.0, 0.0).astype(BF16)
    tags = jnp.dot(
        step_hot,
        jnp.where(placed, local + 1.0, 0.0).astype(BF16),
        preferred_element_type=F32,
    )
    for k in range(z.n_dp):
        tags_out[k] = tags[k : k + 1, :]
    tags_copy = [
        remote(
            tags_out.at[k], tags_in.at[k], tags_send.at[k], tags_recv.at[k],
            dp=lax.rem(p + k, z.n_dp),
        )
        for k in range(1, z.n_dp)
    ]

    member_tag[0] = jnp.where(
        member_valid[...] == 1, member_cluster[...].astype(F32) + 1.0, -1.0
    )
    load_members.wait()
    values = raw[...].astype(F32)
    unit[:, 0] = (
        (values / jnp.sqrt(jnp.sum(values * values, axis=1, keepdims=True) + EPSILON))
        .astype(BF16)
        .reshape(2, z.members // 2, z.emb)
    )
    mtag_copy = [
        remote(
            member_tag.at[0], member_tag.at[j], mtag_send.at[j], mtag_recv.at[j],
            tensor=forward_of(j),
        )
        for j in range(1, z.n_tensor)
    ]

    def head(first, last):
        count = last - first
        total = jnp.dot(
            feat[0, first:last].reshape(count * z.rows, half),
            w1[:half, :],
            preferred_element_type=F32,
        )
        total += jnp.dot(
            feat[1, first:last].reshape(count * z.rows, half),
            w1[half:, :],
            preferred_element_type=F32,
        )
        hidden = jax.nn.gelu(total).astype(BF16)
        for c in range(CHUNKS):
            sums_out[c, first:last] = (
                jnp.dot(
                    hidden, w2[:, c * z.cols : (c + 1) * z.cols], preferred_element_type=F32
                )
                .astype(BF16)
                .reshape(count, z.rows, z.cols)
            )
            for j in range(max(first, 1), last):
                sums_copy[c, j] = remote(
                    sums_out.at[c, j], sums_in.at[c, j], sums_send.at[c, j], sums_recv.at[c, j],
                    tensor=source_of(j),
                )

    sums_copy = {}
    for copy in (*own, *load_w1, load_w2):
        copy.wait()
    head(0, 1)

    for j in along_x:
        feat_copy[0, j].wait_recv()
        for y in along_y:
            send_feature(0, corner(j, y), feat.at[0, j], y)
    for j in along_y:
        feat_copy[1, j].wait_recv()
        for x in along_x:
            send_feature(1, corner(x, j), feat.at[1, j], x)
    for j in along_x:
        feat_copy[1, j].wait_recv()
    for j in along_y:
        feat_copy[0, j].wait_recv()
    head(1, 1 + len(along_x) + len(along_y))
    for j in far:
        feat_copy[0, j].wait_recv()
        feat_copy[1, j].wait_recv()

    unit_copy = {}

    def send_unit(h, j, held, target):
        unit_copy[h, j] = remote(
            unit.at[h, held], unit.at[h, j], unit_send.at[h, j], unit_recv.at[h, j],
            tensor=forward_of(target),
        )

    if far:
        head(far[0], far[-1] + 1)

    code = step_row * float(z.cap) + rank_row
    code = code.reshape(1, 1, rows)
    if z.whole:
        shape = (z.n_dp, z.whole, rows)
        pack_whole = jnp.where(
            code == iota(shape, 0) * float(z.cap) + iota(shape, 1), 1.0, 0.0
        ).reshape(z.n_dp * z.whole, rows).astype(BF16)
    pack_rest = []
    if z.rest:
        shape = (z.n_dp, z.folded, rows)
        for c in range(z.tiles):
            at = iota(shape, 1) - float(c * z.rest)
            inside = (at >= 0.0) & (at < float(z.rest))
            hit = inside & (code == iota(shape, 0) * float(z.cap) + float(z.whole) + at)
            pack_rest.append(
                jnp.where(hit, 1.0, 0.0).reshape(z.n_dp * z.folded, rows).astype(BF16)
            )

    square = jnp.zeros((rows, 1), F32)
    docs_copy = {}
    for c in range(CHUNKS):
        proj = sums_out[c, 0].astype(F32)
        for j in range(1, z.n_tensor):
            sums_copy[c, j].wait_recv()
            proj += sums_in[c, j].astype(F32)
        query = proj.astype(BF16)
        if z.whole:
            packed = jnp.dot(pack_whole, query, preferred_element_type=F32).astype(BF16)
        if z.rest:
            tail = jnp.zeros((z.n_dp * z.folded, 128), F32)
            for i in range(z.tiles):
                tail += jnp.dot(
                    pack_rest[i], query[:, i * 128 : (i + 1) * 128], preferred_element_type=F32
                )
            tail = tail.astype(BF16)
        for k in [*range(1, z.n_dp), 0]:
            target = docs_out if k else docs_in
            if z.whole:
                for i in range(z.tiles):
                    target[c, k, i * z.whole : (i + 1) * z.whole, :] = packed[
                        k * z.whole : (k + 1) * z.whole, i * 128 : (i + 1) * 128
                    ]
            if z.rest:
                target[c, k, z.tiles * z.whole :, :] = tail[k * z.folded : (k + 1) * z.folded, :]
            if k:
                docs_copy[c, k] = remote(
                    docs_out.at[c, k], docs_in.at[c, k], docs_send.at[c, k], docs_recv.at[c, k],
                    dp=lax.rem(p + k, z.n_dp),
                )
        square += jnp.sum(proj * proj, axis=1, keepdims=True)
    for first in (0, 1):
        for j in along_x:
            send_unit(first, j, 0, j)
        for j in along_y:
            send_unit(1 - first, j, 0, j)
    inverse = 1.0 / jnp.sqrt(square + EPSILON)
    for j in along_x:
        unit_copy[0, j].wait_recv()
        for y in along_y:
            send_unit(0, corner(j, y), j, y)
    for j in along_y:
        unit_copy[1, j].wait_recv()
        for x in along_x:
            send_unit(1, corner(x, j), j, x)

    tag_row = tags_out[0]
    for k in range(1, z.n_dp):
        tags_copy[k - 1].wait_recv()
        tag_row += tags_in[k]
    tag_row = tag_row[:, : z.slots]
    for copy in mtag_copy:
        copy.wait_recv()
    allowed = [to_column(member_tag[j], z.members) for j in range(z.n_tensor)]

    unfold = []
    if z.rest:
        shape = (z.n_dp * z.rest, z.n_dp * z.folded)
        out_row, in_row = iota(shape, 0), iota(shape, 1)
        for i in range(z.tiles):
            hit = jnp.zeros(shape, F32)
            for k in range(z.n_dp):
                at = out_row - float(k * z.rest)
                inside = (at >= 0.0) & (at < float(z.rest))
                hit = jnp.where(
                    inside & (in_row == at + float(k * z.folded + i * z.rest)), 1.0, hit
                )
            unfold.append(hit.astype(BF16))

    arrived = []
    for c in range(CHUNKS):
        for k in range(1, z.n_dp):
            docs_copy[c, k].wait_recv()
        parts = []
        if z.whole:
            parts.append(
                jnp.concatenate(
                    [
                        docs_in[c, :, i * z.whole : (i + 1) * z.whole, :].reshape(
                            z.n_dp * z.whole, 128
                        )
                        for i in range(z.tiles)
                    ],
                    axis=1,
                )
            )
        if z.rest:
            tail = docs_in[c, :, z.tiles * z.whole :, :].reshape(z.n_dp * z.folded, 128)
            parts.append(
                jnp.concatenate(
                    [
                        jnp.dot(unfold[i], tail, preferred_element_type=F32).astype(BF16)
                        for i in range(z.tiles)
                    ],
                    axis=1,
                )
            )
        arrived.append(jnp.concatenate(parts, axis=0) if len(parts) > 1 else parts[0])
    top = jnp.full((1, z.slots), LOWEST, F32)
    for j in range(z.n_tensor):
        if j in along_x:
            unit_copy[1, j].wait_recv()
        elif j in along_y:
            unit_copy[0, j].wait_recv()
        elif j:
            unit_copy[0, j].wait_recv()
            unit_copy[1, j].wait_recv()
        scores = jnp.zeros((z.members, z.slots), F32)
        for c in range(CHUNKS):
            scores += lax.dot_general(
                unit[:, j, :, c * z.cols : (c + 1) * z.cols].reshape(z.members, z.cols),
                arrived[c],
                (((1,), (1,)), ((), ())),
                preferred_element_type=F32,
            )
        kept = jnp.where(allowed[j] == tag_row, scores, LOWEST)
        top = jnp.maximum(top, jnp.max(kept, axis=0, keepdims=True))
    answer_out[...] = jnp.zeros_like(answer_out)
    answer_out[:, : z.slots] = top

    answer_copy = [
        remote(
            answer_out, answer_in.at[k], answer_send.at[k], answer_recv.at[k],
            dp=lax.rem(p + z.n_dp - k, z.n_dp),
        )
        for k in range(1, z.n_dp)
    ]
    found = jnp.where(step == 0.0, answer_out[...], 0.0)
    for k in range(1, z.n_dp):
        answer_copy[k - 1].wait_recv()
        found = jnp.where(step == float(k), answer_in[k], found)
    value = jnp.sum(jnp.where(placed, found, 0.0), axis=1, keepdims=True)
    best[...] = to_row(jnp.maximum(value * inverse, -1.0), rows)
    for copy in sent:
        copy.wait_send()


def body(features, w_hidden, w_embed, members, doc_owner, doc_local, member_cluster, member_valid):
    n_dp, n_tensor = lax.axis_size("dp"), lax.axis_size("tensor")
    rows, hid = features.shape
    width, emb = w_embed.shape
    z = Sizes(n_dp, n_tensor, rows, hid, width, emb, members.shape[1])
    half = hid // 2
    dma = pltpu.SemaphoreType.DMA
    hbm = pl.BlockSpec(memory_space=pl.ANY)
    vmem = pl.BlockSpec(memory_space=pltpu.VMEM)
    out = pl.pallas_call(
        functools.partial(kernel, z),
        out_shape=jax.ShapeDtypeStruct((1, rows), F32),
        in_specs=[hbm] * 8,
        out_specs=vmem,
        scratch_shapes=[
            pltpu.VMEM((2, n_tensor, rows, half), BF16),
            pltpu.VMEM((hid, width), BF16),
            pltpu.VMEM((width, emb), BF16),
            pltpu.VMEM((z.members, emb), BF16),
            pltpu.VMEM((1, doc_owner.shape[0]), jnp.int32),
            pltpu.VMEM(doc_local.shape, jnp.int32),
            pltpu.VMEM((1, z.members), jnp.int32),
            pltpu.VMEM((1, z.members), jnp.int32),
            pltpu.VMEM((2, n_tensor, z.members // 2, emb), BF16),
            pltpu.VMEM((n_tensor, 1, z.members), F32),
            pltpu.VMEM((CHUNKS, n_tensor, rows, z.cols), BF16),
            pltpu.VMEM((CHUNKS, n_tensor, rows, z.cols), BF16),
            pltpu.VMEM((CHUNKS, n_dp, z.block, 128), BF16),
            pltpu.VMEM((CHUNKS, n_dp, z.block, 128), BF16),
            pltpu.VMEM((n_dp, 1, z.lanes), F32),
            pltpu.VMEM((n_dp, 1, z.lanes), F32),
            pltpu.VMEM((1, z.lanes), F32),
            pltpu.VMEM((n_dp, 1, z.lanes), F32),
            dma((10,)),
            dma((2, n_tensor)),
            dma((2, n_tensor)),
            dma((2, n_tensor)),
            dma((2, n_tensor)),
            dma((n_tensor,)),
            dma((n_tensor,)),
            dma((CHUNKS, n_tensor)),
            dma((CHUNKS, n_tensor)),
            dma((CHUNKS, n_dp)),
            dma((CHUNKS, n_dp)),
            dma((n_dp,)),
            dma((n_dp,)),
            dma((n_dp,)),
            dma((n_dp,)),
        ],
        compiler_params=pltpu.CompilerParams(
            collective_id=0, has_side_effects=True, vmem_limit_bytes=62 * 1024 * 1024
        ),
        name="match",
    )(
        features,
        w_hidden,
        w_embed,
        members,
        doc_owner.reshape(1, -1),
        doc_local,
        member_cluster,
        member_valid,
    )
    return out.reshape(rows)


def solution(mesh):
    return jax.shard_map(
        body,
        mesh=mesh,
        in_specs=(
            P(("dp", "tensor"), None),
            P(None, "tensor"),
            P("tensor", None),
            P("dp", "tensor", None),
            P("dp", None),
            P("dp"),
            P("dp", "tensor"),
            P("dp", "tensor"),
        ),
        out_specs=P(("dp", "tensor")),
        check_vma=False,
    )
```

profile of v0, /device:TPU:0, one launch (start us, length us, event | category | flops | bytes accessed | tf_op | source)
XLA Modules:
  0.0 38.7 jit_solution(7215465673583605629)
XLA Ops:
  0.0 37.5 %match.1 = f32[1,80]{1,0:T(1,128)} custom-call(bf16[80,2048]{1,0:T(8,128)(2,1)} %features.1, bf16[2048,512]{1,0:T(8,128)(2,1)} %w_hidden.1, bf16[512,768]{1,0:T(8,128)(2,1)} %w_embed.1, bf16[1,128,768]{2,1,0:T(8,128)(2,1)} %members.1, s32[1,320]{1,0:T(1,128)} %bitcast.2, s32[320]{0:T(512)} %hbm_local.1, s32[1,128]{1,0:T(1,128)} %hbm_cluster.1, ...), custom_call_target="tpu_custom_call" | custom-call | tf_op jit(solution)/shard_map/match/pallas_call | solution.py:458
  37.5 1.2 %copy.10 = f32[80]{0:T(128)} copy(f32[80]{0:T(128)} %bitcast.3) | data formatting | bytes 640
where the time goes:
time: 38.8 us; the launch traced here: 38.7 us
  Pallas kernels  37.5 us (97%)
  local copies, waits for them, and re-layouts  1.19 us (3%)
    pallas_call x1, Pallas kernels, body(): pl.pallas_call(functools.partial(kernel, z), out_shape=jax.ShapeDtypeStru...  37.5 us
    unnamed x1, local copies, waits for them, and re-layouts  1.19 us

commit v1 on v0

--- a/solution.py
+++ b/solution.py
@@ -242,26 +242,23 @@
             w1[half:, :],
             preferred_element_type=F32,
         )
-        hidden = jax.nn.gelu(total).astype(BF16)
-        for c in range(CHUNKS):
-            sums_out[c, first:last] = (
-                jnp.dot(
-                    hidden, w2[:, c * z.cols : (c + 1) * z.cols], preferred_element_type=F32
-                )
-                .astype(BF16)
-                .reshape(count, z.rows, z.cols)
+        return jax.nn.gelu(total).astype(BF16)
+
+    def embed(hidden, c, first, last):
+        sums_out[c, first:last] = (
+            jnp.dot(hidden, w2[:, c * z.cols : (c + 1) * z.cols], preferred_element_type=F32)
+            .astype(BF16)
+            .reshape(last - first, z.rows, z.cols)
+        )
+
+    def send_sums(c, first, last):
+        for j in range(first, last):
+            sums_copy[c, j] = remote(
+                sums_out.at[c, j], sums_in.at[c, j], sums_send.at[c, j], sums_recv.at[c, j],
+                tensor=source_of(j),
             )
-            for j in range(max(first, 1), last):
-                sums_copy[c, j] = remote(
-                    sums_out.at[c, j], sums_in.at[c, j], sums_send.at[c, j], sums_recv.at[c, j],
-                    tensor=source_of(j),
-                )
 
     sums_copy = {}
-    for copy in (*own, *load_w1, load_w2):
-        copy.wait()
-    head(0, 1)
-
     for j in along_x:
         feat_copy[0, j].wait_recv()
         for y in along_y:
@@ -270,14 +267,33 @@
         feat_copy[1, j].wait_recv()
         for x in along_x:
             send_feature(1, corner(x, j), feat.at[1, j], x)
+    for copy in (*own, *load_w1, load_w2):
+        copy.wait()
+    hidden = head(0, 1)
+    for c in range(CHUNKS):
+        embed(hidden, c, 0, 1)
+
+    near = 1 + len(along_x) + len(along_y)
     for j in along_x:
         feat_copy[1, j].wait_recv()
     for j in along_y:
         feat_copy[0, j].wait_recv()
-    head(1, 1 + len(along_x) + len(along_y))
+    if near > 1:
+        hidden = head(1, near)
+        for c in range(CHUNKS):
+            embed(hidden, c, 1, near)
     for j in far:
         feat_copy[0, j].wait_recv()
         feat_copy[1, j].wait_recv()
+    send_sums(0, 1, near)
+    if far:
+        hidden = head(near, z.n_tensor)
+    for c in range(CHUNKS):
+        if c:
+            send_sums(c, 1, near)
+        if far:
+            embed(hidden, c, near, z.n_tensor)
+            send_sums(c, near, z.n_tensor)
 
     unit_copy = {}
 
@@ -286,9 +302,6 @@
             unit.at[h, held], unit.at[h, j], unit_send.at[h, j], unit_recv.at[h, j],
             tensor=forward_of(target),
         )
-
-    if far:
-        head(far[0], far[-1] + 1)
 
     code = step_row * float(z.cap) + rank_row
     code = code.reshape(1, 1, rows)
@@ -340,11 +353,12 @@
                     dp=lax.rem(p + k, z.n_dp),
                 )
         square += jnp.sum(proj * proj, axis=1, keepdims=True)
-    for first in (0, 1):
-        for j in along_x:
-            send_unit(first, j, 0, j)
-        for j in along_y:
-            send_unit(1 - first, j, 0, j)
+        if c == 0:
+            for first in (0, 1):
+                for j in along_x:
+                    send_unit(first, j, 0, j)
+                for j in along_y:
+                    send_unit(1 - first, j, 0, j)
     inverse = 1.0 / jnp.sqrt(square + EPSILON)
     for j in along_x:
         unit_copy[0, j].wait_recv()
@@ -457,7 +471,7 @@
     vmem = pl.BlockSpec(memory_space=pltpu.VMEM)
     out = pl.pallas_call(
         functools.partial(kernel, z),
-        out_shape=jax.ShapeDtypeStruct((1, rows), F32),
+        out_shape=pltpu.VMEM((1, rows), F32),
         in_specs=[hbm] * 8,
         out_specs=vmem,
         scratch_shapes=[

time: 38.8 us -> 37.9 us (0.977)
  local copies, waits for them, and re-layouts: 1.19 us -> 0.51 us
    unnamed x1, local copies, waits for them, and re-layouts: 1.19 us -> 0.51 us
where the time goes in v1:
time: 37.9 us; the launch traced here: 37.8 us
  Pallas kernels  37.3 us (98%)
  local copies, waits for them, and re-layouts  0.51 us (1%)
    pallas_call x1, Pallas kernels, body(): pl.pallas_call(functools.partial(kernel, z), out_shape=pltpu.VMEM((1, row...  37.3 us

profile of v1, /device:TPU:0, one launch (start us, length us, event | category | flops | bytes accessed | tf_op | source)
XLA Modules:
  0.0 37.8 jit_solution(2453363926578380170)
XLA Ops:
  0.0 37.3 %match.1 = f32[1,80]{1,0:T(1,128)S(1)} custom-call(bf16[80,2048]{1,0:T(8,128)(2,1)} %features.1, bf16[2048,512]{1,0:T(8,128)(2,1)} %w_hidden.1, bf16[512,768]{1,0:T(8,128)(2,1)} %w_embed.1, bf16[1,128,768]{2,1,0:T(8,128)(2,1)} %members.1, s32[1,320]{1,0:T(1,128)} %bitcast.3, s32[320]{0:T(512)} %hbm_local.1, s32[1,128]{1,0:T(1,128)} %hbm_cluster.1, ...), custom_call_target="tpu_custom_call" | custom-call | tf_op jit(solution)/shard_map/match/pallas_call | solution.py:472
  37.3 0.5 %copy.10 = f32[80]{0:T(128)} copy(f32[80]{0:T(128)S(1)} %bitcast.2) | data formatting | bytes 640
